TPU v7x, 32 devices: a whole 2x2x4 slice. The times are simulated.
32 devices in a mesh: groups: 2 (over y), seq: 16 (over z, x, core).
Axes of the slice: x: 2, y: 2, z: 4, core: 2. Of those that a mesh axis runs over, the one named last changes fastest.
Arguments:
- hidden_now: bfloat16 [4096, 1792], P(('groups', 'seq')), parts along dimension 0, may hold values from -4 to 4
- stale_rows: bfloat16 [4096, 1792], P(('groups', 'seq')), parts along dimension 0, may hold values from -6 to 6
- expert_ids: int32 [4096, 2], P(('groups', 'seq')), parts along dimension 0, may hold values from 0 to 15, all different within a row; in each aligned block of 128 rows (0 to 127, 128 to 255, ...) at most 20 rows name the same one
- condition: float32 [3584], P('groups'), parts along dimension 0, may hold values from -5 to 5
- mod_weight: bfloat16 [1792, 5376], P(None, 'seq'), may hold values from -0.125 to 0.125
- mod_bias: float32 [5376], P('seq'), may hold values from -3 to 3
- router: bfloat16 [1792, 16], replicated, may hold values from -0.25 to 0.25
- w_gate: bfloat16 [1792, 57344], P(None, 'seq'), may hold values from -0.125 to 0.125
- w_up: bfloat16 [1792, 57344], P(None, 'seq'), may hold values from -0.125 to 0.125
- w_down: bfloat16 [57344, 1792], P('seq'), may hold values from -0.09375 to 0.09375
Outputs:
- mixed: bfloat16 [4096, 1792], P(('groups', 'seq')), parts along dimension 0
There are 2 independent parts, one for each index of `groups`. A program takes and returns all parts, laid end to end along the dimension named above; an argument that names none is the same for every part. Nothing has to cross between parts.
Inputs may be any that keep to these rules, and one draw needn't show every extreme that they name: `expert_ids`: each token names 2 different experts. Within the 128 tokens of one aligned block no expert is named more than 20 times, and in every draw some block names some expert exactly 20 times.
All inputs are finite; a program needn't handle non-finite values.
Results may differ from a plain program's by a relative error of at most 0.0058.
Values may be sent and summed in bfloat16 or wider, within the bound.
A program may use at most 128 MiB of HBM per device.

v0:
```python
import jax
import jax.numpy as jnp
from jax import lax
from jax.sharding import PartitionSpec as P

EXPERTS = 16
TOP = 2
CAP = 20


def token_slots(block_ids):
    flat_ids = block_ids.reshape(-1)
    expert_range = jnp.arange(EXPERTS, dtype=jnp.int32)
    onehot = (flat_ids[:, None] == expert_range[None, :]).astype(jnp.int32)
    counts = jnp.cumsum(onehot, axis=0) - 1
    return jnp.sum(onehot * counts, axis=1).reshape(block_ids.shape)


def local(
    hidden_now,
    stale_rows,
    expert_ids,
    condition,
    mod_weight,
    mod_bias,
    router,
    w_gate,
    w_up,
    w_down,
):
    model_width = hidden_now.shape[1]
    tok_rows = hidden_now.shape[0]
    conditioned = jax.nn.silu(condition).astype(jnp.bfloat16)[None, :]
    mod_piece = jnp.dot(conditioned, mod_weight, preferred_element_type=jnp.float32)[0] + mod_bias
    modulation = lax.all_gather(mod_piece, "seq", axis=0, tiled=True)
    shift_part = modulation[:model_width]
    scale_part = modulation[model_width : 2 * model_width]
    gate_part = modulation[2 * model_width :]
    stream = hidden_now.astype(jnp.float32)
    row_mean = jnp.mean(stream, axis=-1, keepdims=True)
    centered = stream - row_mean
    variance = jnp.mean(centered * centered, axis=-1, keepdims=True)
    normed = centered * lax.rsqrt(variance + 1e-06)
    current = (normed * (1.0 + scale_part) + shift_part).astype(jnp.bfloat16)
    logits = jnp.dot(current, router, preferred_element_type=jnp.float32)
    picked = jnp.take_along_axis(logits, expert_ids, axis=1)
    weights = jax.nn.sigmoid(picked - picked[:, ::-1])
    slot_index = token_slots(expert_ids)
    position = expert_ids * CAP + slot_index
    slot_table = jnp.arange(EXPERTS * CAP, dtype=jnp.int32)
    selector = jnp.any(position[None, :, :] == slot_table[:, None, None], axis=2).astype(
        jnp.bfloat16
    )
    dispatched = jnp.dot(selector, stale_rows, preferred_element_type=jnp.float32).astype(
        jnp.bfloat16
    )
    devices = lax.axis_size("seq")
    group_size = devices // EXPERTS
    outgoing = jnp.broadcast_to(
        dispatched.reshape(EXPERTS, 1, CAP, model_width), (EXPERTS, group_size, CAP, model_width)
    )
    outgoing = outgoing.reshape(devices, CAP, model_width)
    received_rows = lax.all_to_all(outgoing, "seq", split_axis=0, concat_axis=0, tiled=True)
    sources, count, feats = received_rows.shape
    flat_rows = received_rows.reshape(sources * count, feats)
    gate_val = jnp.dot(flat_rows, w_gate, preferred_element_type=jnp.float32)
    up_val = jnp.dot(flat_rows, w_up, preferred_element_type=jnp.float32)
    activation = (jax.nn.silu(gate_val) * up_val).astype(jnp.bfloat16)
    partial_out = jnp.dot(activation, w_down, preferred_element_type=jnp.float32)
    returned = lax.all_to_all(
        partial_out.astype(jnp.bfloat16).reshape(sources, count, feats),
        "seq",
        split_axis=0,
        concat_axis=0,
        tiled=True,
    )
    expert_out = jnp.sum(
        returned.reshape(EXPERTS, group_size, CAP, model_width).astype(jnp.float32), axis=1
    )
    expert_out = expert_out.reshape(EXPERTS * CAP, model_width)
    token_rows = jnp.take(expert_out, position.reshape(-1), axis=0).reshape(
        tok_rows, TOP, model_width
    )
    routed = jnp.sum(weights[:, :, None] * token_rows, axis=1)
    return (stream + gate_part * routed).astype(jnp.bfloat16)


def solution(mesh):
    in_specs = (
        P(("groups", "seq"), None),
        P(("groups", "seq"), None),
        P(("groups", "seq"), None),
        P("groups"),
        P(None, "seq"),
        P("seq"),
        P(),
        P(None, "seq"),
        P(None, "seq"),
        P("seq", None),
    )
    out_specs = P(("groups", "seq"), None)
    return jax.shard_map(local, mesh=mesh, in_specs=in_specs, out_specs=out_specs, check_vma=False)
```

profile of v0, /device:TPU:0, one launch (start us, length us, event | category | flops | bytes accessed | tf_op | source)
XLA Modules:
  0.0 176.3 jit_solution(11989287611082827127)
XLA Ops:
  0.0 0.9 copy.38
  0.9 0.1 eq.42
  1.0 0.1 eq.38
  1.2 0.6 reduce-window.6
  1.8 0.2 slice_reduce_fusion
  2.1 0.1 reshape.114
  2.3 0.7 compare_and_fusion
  3.1 1.5 convolution_convert_fusion
  4.6 1.2 reshape_reshape.3
  5.8 7.4 %all-to-all-start = ((bf16[16,20,1792]{2,1,0:T(8,128)(2,1)}), bf16[16,20,1792]{2,1,0:T(8,128)(2,1)S(1)}, u32[]{:S(2)}, u32[]{:S(2)}) async-start(bf16[16,20,1792]{2,1,0:T(8,128)(2,1)} %reshape_reshape.3), calls=%async_computation | async-start | bytes 2752512 | tf_op jit(solution)/shard_map/all_to_all | solution.py:63
  13.3 0.1 reshape.119
  13.6 0.1 reshape.130
  13.7 0.6 dynamic-slice
  15.0 0.5 convolution_reduce_fusion
  15.5 26.2 %all-to-all-done = bf16[16,20,1792]{2,1,0:T(8,128)(2,1)S(1)} async-done(((bf16[16,20,1792]{2,1,0:T(8,128)(2,1)}), bf16[16,20,1792]{2,1,0:T(8,128)(2,1)S(1)}, u32[]{:S(2)}, u32[]{:S(2)}) %all-to-all-start) | async-done | bytes 1146912 | tf_op jit(solution)/shard_map/all_to_all | solution.py:63
  41.7 1.2 reshape.115
  42.9 11.4 %fusion.16 = f32[320,3584]{1,0:T(8,128)} fusion(bf16[320,1792]{1,0:T(8,128)(2,1)} %reshape.115, bf16[1792,3584]{1,0:T(8,128)(2,1)} %param.17), kind=kOutput, calls=%fused_computation.45 | convolution fusion | flops 4110417920 | bytes 18579456 | tf_op jit(solution)/shard_map/dot_general | solution.py:66
  54.3 18.5 %convolution_convert_fusion.1 = bf16[320,1792]{1,0:T(8,128)(2,1)S(1)} fusion(bf16[3584,1792]{1,0:T(8,128)(2,1)} %param.19, bf16[320,1792]{1,0:T(8,128)(2,1)S(1)} %copy-done.3, bf16[1792,3584]{1,0:T(8,128)(2,1)} %param.18, f32[320,3584]{1,0:T(8,128)} %fusion.16), kind=kOutput, calls=%fused_computation.5 | convolution fusion | flops 8228290560 | bytes 32571392 | tf_op jit(solution)/shard_map/dot_general | solution.py:69
  72.8 1.2 reshape.116
  74.1 8.4 %all-to-all-start.1 = ((bf16[16,20,1792]{2,1,0:T(8,128)(2,1)}), bf16[16,20,1792]{2,1,0:T(8,128)(2,1)}, u32[]{:S(2)}, u32[]{:S(2)}) async-start(bf16[16,20,1792]{2,1,0:T(8,128)(2,1)} %reshape.116), calls=%async_computation.1 | async-start | bytes 2752512 | tf_op jit(solution)/shard_map/all_to_all | solution.py:70
  82.7 78.6 %all-reduce = f32[5376]{0:T(1024)S(1)} all-reduce(f32[5376]{0:T(1024)S(1)} %add_dynamic-update-slice_fusion), channel_id=1, replica_groups=mesh['groups'=2,'seq'=16] {'seq'}, use_global_device_ids=true, to_apply=%add | all-reduce | flops 5376 | bytes 43008
  161.3 0.1 convert_reduce_fusion
  161.5 0.3 fusion.3
  161.8 0.3 fusion.8
  162.1 2.0 %gather_fusion.1 = f32[256]{0:T(256)S(1)} fusion(f32[128,16]{0,1:T(8,128)S(1)} %fusion.8, s32[256]{0:T(256)S(1)} %reshape.130), kind=kCustom, calls=%fused_computation.1 | custom fusion | bytes 4096 | tf_op jit(solution)/shard_map/jit(take_along_axis)/gather | solution.py:46
  164.4 0.8 copy.37
  165.1 0.1 copy.42
  165.3 1.4 reshape.121
  166.7 2.6 %gather_fusion = f32[256,1792]{1,0:T(8,128)} fusion(f32[320,1792]{1,0:T(8,128)S(1)} %reshape.121, s32[1024]{0:T(1024)S(1)} %pad_clamp_fusion), kind=kCustom, calls=%fused_computation | custom fusion | bytes 3671040 | tf_op jit(solution)/shard_map/jit(_take)/gather | solution.py:81
  169.4 2.4 %gather.12 = f32[128,2,1792]{2,1,0:T(2,128)S(1)} reshape(f32[256,1792]{1,0:T(8,128)} %gather_fusion) | data formatting | bytes 3670016 | tf_op jit(solution)/shard_map/jit(_take)/gather | solution.py:81
  171.8 3.6 %multiply_reduce_fusion = f32[128,1792]{1,0:T(8,128)S(1)} fusion(f32[128,2,1792]{2,1,0:T(2,128)S(1)} %gather.12, pred[128,2]{1,0:T(8,128)(4,1)S(1)} %copy.42, f32[128,2]{1,0:T(8,128)S(1)} %copy-done.4), kind=kLoop, calls=%fused_computation.6 | loop fusion | flops 1146880 | bytes 2753792 | tf_op jit(solution)/shard_map/reduce_sum | solution.py:84
  175.5 0.9 fusion.7
  (44 shorter events, 1.0 us)
Async XLA Ops:
  0.0 15.0 %copy-start = (bf16[1792,336]{0,1:T(8,128)(2,1)S(1)}, bf16[1792,336]{0,1:T(8,128)(2,1)}, u32[]{:S(2)}) copy-start(bf16[1792,336]{0,1:T(8,128)(2,1)} %param.14) | copy-start | bytes 3612676
  4.5 8.9 %copy-start.6 = (f32[1792]{0:T(1024)S(1)}, f32[1792]{0:T(1024)}, u32[]{:S(2)}) copy-start(f32[1792]{0:T(1024)} %param.13) | copy-start | bytes 21508
  4.5 8.9 %copy-start.5 = (s32[128,2]{0,1:T(2,128)S(1)}, s32[128,2]{0,1:T(2,128)}, u32[]{:S(2)}) copy-start(s32[128,2]{0,1:T(2,128)} %param.12) | copy-start | bytes 3076
  4.5 9.2 %copy-start.9 = (u32[32]{0:T(128)S(1)}, u32[32]{0:T(128)}, u32[]{:S(2)}) copy-start(u32[32]{0:T(128)} %constant.72) | copy-start | bytes 388
  5.8 35.9 %all-to-all-start = ((bf16[16,20,1792]{2,1,0:T(8,128)(2,1)}), bf16[16,20,1792]{2,1,0:T(8,128)(2,1)S(1)}, u32[]{:S(2)}, u32[]{:S(2)}) async-start(bf16[16,20,1792]{2,1,0:T(8,128)(2,1)} %reshape_reshape.3), calls=%async_computation | async-start | bytes 2752512 | tf_op jit(solution)/shard_map/all_to_all | solution.py:63
  42.9 11.4 %copy-start.3 = (bf16[320,1792]{1,0:T(8,128)(2,1)S(1)}, bf16[320,1792]{1,0:T(8,128)(2,1)}, u32[]{:S(2)}) copy-start(bf16[320,1792]{1,0:T(8,128)(2,1)} %reshape.115) | copy-start | bytes 3440644
  72.8 9.7 %copy-start.7 = (f32[336]{0:T(512)S(1)}, f32[336]{0:T(512)}, u32[]{:S(2)}) copy-start(f32[336]{0:T(512)} %param.15) | copy-start | bytes 4036
  72.8 88.5 %copy-start.1 = (bf16[128,1792]{1,0:T(8,128)(2,1)S(1)}, bf16[128,1792]{1,0:T(8,128)(2,1)}, u32[]{:S(2)}) copy-start(bf16[128,1792]{1,0:T(8,128)(2,1)} %param.10) | copy-start | bytes 1376260
  74.1 87.7 %copy-start.8 = (bf16[1792,16]{0,1:T(8,128)(2,1)S(1)}, bf16[1792,16]{0,1:T(8,128)(2,1)}, u32[]{:S(2)}) copy-start(bf16[1792,16]{0,1:T(8,128)(2,1)} %param.16) | copy-start | bytes 172036
  74.1 91.2 %all-to-all-start.1 = ((bf16[16,20,1792]{2,1,0:T(8,128)(2,1)}), bf16[16,20,1792]{2,1,0:T(8,128)(2,1)}, u32[]{:S(2)}, u32[]{:S(2)}) async-start(bf16[16,20,1792]{2,1,0:T(8,128)(2,1)} %reshape.116), calls=%async_computation.1 | async-start | bytes 2752512 | tf_op jit(solution)/shard_map/all_to_all | solution.py:70
  169.4 2.4 %copy-start.4 = (f32[128,2]{1,0:T(8,128)S(1)}, f32[128,2]{1,0:T(8,128)}, u32[]{:S(2)}) copy-start(f32[128,2]{1,0:T(8,128)} %copy.37) | copy-start | bytes 3076
  171.8 3.6 %copy-start.2 = (bf16[128,1792]{1,0:T(8,128)(2,1)S(1)}, bf16[128,1792]{1,0:T(8,128)(2,1)}, u32[]{:S(2)}) copy-start(bf16[128,1792]{1,0:T(8,128)(2,1)} %param.10) | copy-start | bytes 1376260
where the time goes:
time: 177 us; the launch traced here: 176 us
  blocking collectives  78.6 us (44%)
  matrix products  32.2 us (18%)
  waiting for transfers between devices  26.3 us (15%)
  local copies, waits for them, and re-layouts  16 us (9%)
  starting transfers between devices  15.8 us (9%)
  other arithmetic  6.57 us (4%)
    unnamed x1, blocking collectives  78.6 us
    all_to_all x1, waiting for transfers between devices, local(): lax.all_to_all(outgoing, 'seq', split_axis=0, concat_axis=0, tiled=True)  26.2 us
    dot_general x1, matrix products, local(): jnp.dot(activation, w_down, preferred_element_type=jnp.float32)  18.5 us
    dot_general x1, matrix products, local(): gate_val = jnp.dot(flat_rows, w_gate, preferred_element_type=jnp.float32)  11.4 us
    all_to_all x1, starting transfers between devices, local(): lax.all_to_all(partial_out.astype(jnp.bfloat16).reshape(sources, count, f...  8.45 us
    all_to_all x1, starting transfers between devices, local(): lax.all_to_all(outgoing, 'seq', split_axis=0, concat_axis=0, tiled=True)  7.36 us
    gather x2, local copies, waits for them, and re-layouts, local(): jnp.take(expert_out, position.reshape(-1), axis=0)  5.06 us
    reduce_sum x1, other arithmetic, local(): routed = jnp.sum(weights[:, :, None] * token_rows, axis=1)  3.61 us
  transfers between devices with their start and end apart: 2, of which 1 were waited for; matrix products, arithmetic and copies ran while one was open for 3% of the time, Pallas kernels for 0%

commit v1 on v0

v1 whole, which is shorter than its diff:
```python
import functools

import jax
import jax.numpy as jnp
from jax import lax
from jax.experimental import pallas as pl
from jax.experimental.pallas import tpu as pltpu
from jax.sharding import PartitionSpec as P

EXPERTS = 16
TOP = 2
CAP = 20
BASE = 16
REST = CAP - BASE
PARTS = BASE // REST
PIECE = 512
CHUNKS = 4
MESH = pl.DeviceIdType.MESH


def pieces(width):
    return [(q, q * PIECE, min(PIECE, width - q * PIECE)) for q in range(PARTS)]


def keys_of(ids):
    rows = ids.shape[0]
    experts = lax.broadcasted_iota(jnp.int32, (rows, EXPERTS), 1)
    hot = [(ids[:, k : k + 1] == experts).astype(jnp.float32) for k in range(TOP)]
    below = (
        lax.broadcasted_iota(jnp.int32, (rows, rows), 1)
        < lax.broadcasted_iota(jnp.int32, (rows, rows), 0)
    ).astype(jnp.bfloat16)
    before = jnp.dot(
        below, (hot[0] + hot[1]).astype(jnp.bfloat16), preferred_element_type=jnp.float32
    )
    main, rest = [], []
    for k in range(TOP):
        slot = jnp.sum(hot[k] * before, axis=1, keepdims=True).astype(jnp.int32)
        first = ids[:, k : k + 1] * BASE + slot
        main.append(jnp.where(slot < BASE, first, -1))
        rest.append(jnp.where(slot >= BASE, first - BASE, -(EXPERTS + 1) * BASE))
    return hot, main, rest


def onehot(key, table):
    return (key == table).astype(jnp.float32).astype(jnp.bfloat16)


def exchange(
    n, ff_tile, d_tile, ids_ref, stale_ref, wg_hbm, wu_hbm, wd_hbm, out_ref,
    wg, wu, wd, send, recv, ret, xbuf, act,
    w_sem, out_sem, in_sem, back_sem, home_sem,
):
    width = stale_ref.shape[1]
    ff = wg.shape[1]
    group = n // EXPERTS
    half = n // 2
    per = n // CHUNKS
    me = lax.axis_index("seq")
    mine = lax.axis_index("groups")
    side, place = me // half, me % half

    loads = [
        pltpu.make_async_copy(src, dst, w_sem.at[i])
        for i, (src, dst) in enumerate(((wg_hbm, wg), (wu_hbm, wu), (wd_hbm, wd)))
    ]

    def target(k):
        far = (1 - side) * half + (place + k) % half
        near = side * half + (place + k) % half
        return jnp.where(k < half, far, near)

    def source(k):
        far = (1 - side) * half + (place + 2 * half - k) % half
        near = side * half + (place + 2 * half - k) % half
        return jnp.where(k < half, far, near)

    def rows(k):
        return pl.ds(pl.multiple_of(k * BASE, BASE), BASE)

    def outward(k):
        to = target(k)
        return pltpu.make_async_remote_copy(
            src_ref=send.at[rows(to // group)],
            dst_ref=recv.at[rows(k)],
            send_sem=out_sem.at[k],
            recv_sem=in_sem.at[k],
            device_id=(mine, to),
            device_id_type=MESH,
        )

    def homeward(k):
        return pltpu.make_async_remote_copy(
            src_ref=ret.at[rows(k)],
            dst_ref=out_ref.at[rows(me)],
            send_sem=back_sem.at[k],
            recv_sem=home_sem.at[me],
            device_id=(mine, source(k)),
            device_id_type=MESH,
        )

    barrier = pltpu.get_barrier_semaphore()

    @pl.loop(1, n)
    def _(t):
        pl.semaphore_signal(
            barrier, inc=1, device_id=(mine, (me + t) % n), device_id_type=MESH
        )

    _, main, rest = keys_of(ids_ref[...])
    stale = stale_ref[...]
    table = lax.broadcasted_iota(jnp.int32, (stale.shape[0], EXPERTS * BASE), 1)
    over_rows = (((0,), (0,)), ((), ()))
    pick = onehot(main[0], table) + onehot(main[1], table)
    send[:, :width] = lax.dot_general(
        pick, stale, over_rows, preferred_element_type=jnp.float32
    ).astype(jnp.bfloat16)
    tail = jnp.zeros((EXPERTS * BASE, PIECE), jnp.float32)
    for q, first, size in pieces(width):
        pick = onehot(rest[0] + q * REST, table) + onehot(rest[1] + q * REST, table)
        part = lax.dot_general(
            pick, stale[:, first : first + size], over_rows, preferred_element_type=jnp.float32
        )
        if size < PIECE:
            part = jnp.concatenate(
                [part, jnp.zeros((part.shape[0], PIECE - size), jnp.float32)], axis=1
            )
        tail = tail + part
    send[:, width:] = tail.astype(jnp.bfloat16)

    pl.semaphore_wait(barrier, n - 1)

    @pl.loop(0, half)
    def _(k):
        outward(k).start()

    @pl.loop(half + 1, n)
    def _(k):
        outward(k).start()

    for load in loads:
        load.start()
    recv[pl.ds(half * BASE, BASE), :] = send[rows(me // group), :]

    def work(c):
        base = c * per * BASE
        count = per * BASE
        extra = per * REST
        got = pl.ds(base, count)
        xbuf[:count] = recv[got, :width]
        across = lax.broadcasted_iota(jnp.int32, (extra, count), 1)
        down = lax.broadcasted_iota(jnp.int32, (extra, count), 0)
        spread = (down // REST) * BASE + down % REST
        tails = recv[got, width:]
        for q, first, size in pieces(width):
            xbuf[count:, first : first + size] = jnp.dot(
                onehot(spread + q * REST, across), tails[:, :size],
                preferred_element_type=jnp.float32,
            ).astype(jnp.bfloat16)
        if c == 0:
            loads[0].wait()
            loads[1].wait()

        @pl.loop(0, ff // ff_tile)
        def _(j):
            cols = pl.ds(pl.multiple_of(j * ff_tile, ff_tile), ff_tile)
            gate = jnp.dot(xbuf[...], wg[:, cols], preferred_element_type=jnp.float32)
            up = jnp.dot(xbuf[...], wu[:, cols], preferred_element_type=jnp.float32)
            act[:, cols] = (jax.nn.silu(gate) * up).astype(jnp.bfloat16)

        if c == 0:
            loads[2].wait()

        @pl.loop(0, width // d_tile)
        def _(j):
            cols = pl.ds(pl.multiple_of(j * d_tile, d_tile), d_tile)
            xbuf[:, cols] = jnp.dot(
                act[...], wd[:, cols], preferred_element_type=jnp.float32
            ).astype(jnp.bfloat16)

        ret[got, :width] = xbuf[:count]
        across = lax.broadcasted_iota(jnp.int32, (count, extra), 1)
        down = lax.broadcasted_iota(jnp.int32, (count, extra), 0)
        spread = (across // REST) * BASE + across % REST
        back = jnp.zeros((count, PIECE), jnp.float32)
        for q, first, size in pieces(width):
            part = jnp.dot(
                onehot(spread + q * REST, down), xbuf[count:, first : first + size],
                preferred_element_type=jnp.float32,
            )
            if size < PIECE:
                part = jnp.concatenate(
                    [part, jnp.zeros((count, PIECE - size), jnp.float32)], axis=1
                )
            back = back + part
        ret[got, width:] = back.astype(jnp.bfloat16)

    for c in range(CHUNKS):
        low, high = c * per, (c + 1) * per
        if low == half:
            low = low + 1

        @pl.loop(low, high)
        def _(k):
            outward(k).wait_recv()

        work(c)

        @pl.loop(low, high)
        def _(k):
            homeward(k).start()

        if c * per == half:
            out_ref[rows(me), :] = ret[pl.ds(half * BASE, BASE), :]

    @pl.loop(1, n)
    def _(t):
        d = (me + t) % n
        pltpu.make_async_remote_copy(
            src_ref=ret.at[rows(0)],
            dst_ref=out_ref.at[rows(d)],
            send_sem=back_sem.at[0],
            recv_sem=home_sem.at[d],
            device_id=(mine, d),
            device_id_type=MESH,
        ).wait_recv()

    for low, high in ((0, half), (half + 1, n)):

        @pl.loop(low, high)
        def _(k):
            outward(k).wait_send()
            homeward(k).wait_send()


def combine(group, ids_ref, hidden_ref, mod_ref, router_ref, back_ref, mixed_ref):
    width = hidden_ref.shape[1]
    stream = hidden_ref[...].astype(jnp.float32)
    centered = stream - jnp.mean(stream, axis=-1, keepdims=True)
    variance = jnp.mean(centered * centered, axis=-1, keepdims=True)
    normed = centered * lax.rsqrt(variance + 1e-06)
    shift = mod_ref[:, :width]
    scale = mod_ref[:, width : 2 * width]
    current = (normed * (1.0 + scale) + shift).astype(jnp.bfloat16)
    logits = jnp.dot(current, router_ref[...], preferred_element_type=jnp.float32)
    hot, main, rest = keys_of(ids_ref[...])
    picked = [jnp.sum(hot[k] * logits, axis=1, keepdims=True) for k in range(TOP)]
    row = lax.broadcasted_iota(jnp.int32, (stream.shape[0], back_ref.shape[0]), 1)
    table = (row // (BASE * group)) * BASE + row % BASE
    weights = [jax.nn.sigmoid(picked[k] - picked[1 - k]) for k in range(TOP)]
    whole = [onehot(main[k], table) for k in range(TOP)]
    for q, first, size in pieces(width):
        cols = slice(first, first + size)
        routed = jnp.zeros((stream.shape[0], size), jnp.float32)
        for k in range(TOP):
            found = jnp.dot(whole[k], back_ref[:, cols], preferred_element_type=jnp.float32)
            found = found + jnp.dot(
                onehot(rest[k] + q * REST, table), back_ref[:, width : width + size],
                preferred_element_type=jnp.float32,
            )
            routed = routed + weights[k] * found
        gate = mod_ref[:, 2 * width + first : 2 * width + first + size]
        mixed_ref[:, cols] = (hidden_ref[:, cols].astype(jnp.float32) + gate * routed).astype(
            mixed_ref.dtype
        )


def local(
    hidden_now, stale_rows, expert_ids, condition, mod_weight, mod_bias, router, w_gate, w_up, w_down
):
    n = lax.axis_size("seq")
    width = hidden_now.shape[1]
    ff = w_gate.shape[1]
    ff_tile = 512 if ff % 512 == 0 else ff
    d_tile = 256
    message = width + PIECE
    per = n // CHUNKS
    conditioned = jax.nn.silu(condition).astype(jnp.bfloat16)[None, :]
    mod_piece = jnp.dot(conditioned, mod_weight, preferred_element_type=jnp.float32)[0] + mod_bias
    modulation = lax.all_gather(mod_piece, "seq", axis=0, tiled=True)
    vmem = pl.BlockSpec(memory_space=pltpu.VMEM)
    hbm = pl.BlockSpec(memory_space=pl.ANY)
    bf16 = jnp.bfloat16
    back = pl.pallas_call(
        functools.partial(exchange, n, ff_tile, d_tile),
        out_shape=jax.ShapeDtypeStruct((n * BASE, message), bf16),
        in_specs=[vmem, vmem, hbm, hbm, hbm],
        out_specs=vmem,
        scratch_shapes=[
            pltpu.VMEM(w_gate.shape, bf16),
            pltpu.VMEM(w_up.shape, bf16),
            pltpu.VMEM(w_down.shape, bf16),
            pltpu.VMEM((EXPERTS * BASE, message), bf16),
            pltpu.VMEM((n * BASE, message), bf16),
            pltpu.VMEM((n * BASE, message), bf16),
            pltpu.VMEM((per * CAP, width), bf16),
            pltpu.VMEM((per * CAP, ff), bf16),
            pltpu.SemaphoreType.DMA((3,)),
            pltpu.SemaphoreType.DMA((n,)),
            pltpu.SemaphoreType.DMA((n,)),
            pltpu.SemaphoreType.DMA((n,)),
            pltpu.SemaphoreType.DMA((n,)),
        ],
        compiler_params=pltpu.CompilerParams(
            collective_id=0, has_side_effects=True, vmem_limit_bytes=58 * 1024 * 1024
        ),
        cost_estimate=pl.CostEstimate(
            flops=6 * n * CAP * width * ff, bytes_accessed=6 * width * ff, transcendentals=0
        ),
        name="exchange",
    )(expert_ids, stale_rows, w_gate, w_up, w_down)
    return pl.pallas_call(
        functools.partial(combine, n // EXPERTS),
        out_shape=jax.ShapeDtypeStruct(hidden_now.shape, hidden_now.dtype),
        in_specs=[vmem] * 5,
        out_specs=vmem,
        compiler_params=pltpu.CompilerParams(vmem_limit_bytes=48 * 1024 * 1024),
        name="combine",
    )(expert_ids, hidden_now, modulation[None, :], router, back)


def solution(mesh):
    in_specs = (
        P(("groups", "seq"), None),
        P(("groups", "seq"), None),
        P(("groups", "seq"), None),
        P("groups"),
        P(None, "seq"),
        P("seq"),
        P(),
        P(None, "seq"),
        P(None, "seq"),
        P("seq", None),
    )
    out_specs = P(("groups", "seq"), None)
    return jax.shard_map(local, mesh=mesh, in_specs=in_specs, out_specs=out_specs, check_vma=False)
```

time: 177 us -> 138 us (0.78)
  the two profiles are of different devices: /device:TPU:0 before, /device:TPU:1 now
where the time goes in v1:
time: 138 us; the launch traced here: 136 us
  Pallas kernels  72.5 us (53%)
  blocking collectives  57.9 us (42%)
  local copies, waits for them, and re-layouts  3.66 us (3%)
    pallas_call x1, Pallas kernels, local(): pl.pallas_call(functools.partial(exchange, n, ff_tile, d_tile), out_shape...  70.2 us
    unnamed x1, blocking collectives  57.9 us
    unnamed x18, local copies, waits for them, and re-layouts  3.64 us

profile of v1, /device:TPU:1, one launch (start us, length us, event | category | flops | bytes accessed | tf_op | source)
XLA Modules:
  0.0 136.2 jit_solution(6239411744076950369)
XLA Ops:
  0.0 0.0 copy-start
  0.0 0.0 copy-start.4
  0.0 0.0 copy-start.5
  0.0 0.0 copy-start.6
  0.0 1.3 dynamic-slice
  2.0 0.7 multiply_convert_fusion
  2.7 0.0 copy-done
  2.7 0.5 convolution_reduce_fusion
  3.2 0.0 copy-done.5
  3.2 0.1 add_dynamic-update-slice_fusion
  3.4 57.9 %all-reduce = f32[5376]{0:T(1024)S(1)} all-reduce(f32[5376]{0:T(1024)S(1)} %add_dynamic-update-slice_fusion), channel_id=1, replica_groups=mesh['groups'=2,'seq'=16] {'seq'}, use_global_device_ids=true, to_apply=%add | all-reduce | flops 5376 | bytes 43008
  61.3 0.0 copy-done.6
  61.3 0.7 copy.12.ids_ref
  62.1 0.0 copy-done.4
  62.1 0.3 copy.13.router_ref
  62.3 0.0 copy-start.2
  62.4 0.0 copy-start.3
  62.4 70.2 %exchange.1.back_ref = bf16[256,2304]{1,0:T(8,128)(2,1)} custom-call(s32[128,2]{1,0:T(8,128)} %copy.12.ids_ref, bf16[128,1792]{1,0:T(8,128)(2,1)} %stale_ref.1, bf16[1792,3584]{1,0:T(8,128)(2,1)} %wg_hbm.1, bf16[1792,3584]{1,0:T(8,128)(2,1)} %wu_hbm.1, bf16[3584,1792]{1,0:T(8,128)(2,1)} %wd_hbm.1), custom_call_target="tpu_custom_call" | custom-call | flops 12331253760 | bytes 38535168 | tf_op jit(solution)/shard_map/exchange/pallas_call | solution.py:284
  132.6 0.0 copy-done.2
  132.6 0.0 copy-done.3
  132.6 0.0 copy-start.1
  132.6 1.3 copy-done.1
  133.9 2.3 %combine.1 = bf16[128,1792]{1,0:T(8,128)(2,1)} custom-call(s32[128,2]{1,0:T(8,128)S(1)} %copy-done.3, bf16[128,1792]{1,0:T(8,128)(2,1)S(1)} %copy-done.2, f32[1,5376]{1,0:T(1,128)S(1)} %broadcast_in_dim.4.mod_ref, bf16[1792,16]{1,0:T(8,128)(2,1)S(1)} %copy.13.router_ref, bf16[256,2304]{1,0:T(8,128)(2,1)S(1)} %copy-done.1), custom_call_target="tpu_custom_call" | custom-call | tf_op jit(solution)/shard_map/combine/pallas_call | solution.py:312
  (3 shorter events, 0.0 us)
Async XLA Ops:
  0.0 2.7 %copy-start = (bf16[1792,336]{0,1:T(8,128)(2,1)S(1)}, bf16[1792,336]{0,1:T(8,128)(2,1)}, u32[]{:S(2)}) copy-start(bf16[1792,336]{0,1:T(8,128)(2,1)} %param.14) | copy-start | bytes 3612676
  0.0 62.1 %copy-start.4 = (bf16[1792,16]{0,1:T(8,128)(2,1)S(1)}, bf16[1792,16]{0,1:T(8,128)(2,1)}, u32[]{:S(2)}) copy-start(bf16[1792,16]{0,1:T(8,128)(2,1)} %param.16) | copy-start | bytes 172036
  0.0 3.2 %copy-start.5 = (f32[336]{0:T(512)S(1)}, f32[336]{0:T(512)}, u32[]{:S(2)}) copy-start(f32[336]{0:T(512)} %param.15) | copy-start | bytes 4036
  0.0 61.3 %copy-start.6 = (s32[128,2]{0,1:T(2,128)S(1)}, s32[128,2]{0,1:T(2,128)}, u32[]{:S(2)}) copy-start(s32[128,2]{0,1:T(2,128)} %param.12) | copy-start | bytes 3076
  62.3 70.3 %copy-start.2 = (bf16[128,1792]{1,0:T(8,128)(2,1)S(1)}, bf16[128,1792]{1,0:T(8,128)(2,1)}, u32[]{:S(2)}) copy-start(bf16[128,1792]{1,0:T(8,128)(2,1)} %hidden_ref.1) | copy-start | bytes 1376260
  62.4 70.3 %copy-start.3 = (s32[128,2]{1,0:T(8,128)S(1)}, s32[128,2]{1,0:T(8,128)}, u32[]{:S(2)}) copy-start(s32[128,2]{1,0:T(8,128)} %copy.12.ids_ref) | copy-start | bytes 3076
  132.6 1.3 copy-start.1

commit v2 on v1

--- a/solution.py
+++ b/solution.py
@@ -47,9 +47,10 @@
 
 
 def exchange(
-    n, ff_tile, d_tile, ids_ref, stale_ref, wg_hbm, wu_hbm, wd_hbm, out_ref,
-    wg, wu, wd, send, recv, ret, xbuf, act,
-    w_sem, out_sem, in_sem, back_sem, home_sem,
+    n, ff_tile, d_tile, ids_ref, stale_ref, hidden_ref, cond_ref, bias_ref, router_ref,
+    mw_hbm, wg_hbm, wu_hbm, wd_hbm, mixed_ref,
+    mw, wg, wu, wd, send, recv, ret, out_ref, xbuf, act, mod_own, mod_all,
+    w_sem, out_sem, in_sem, back_sem, home_sem, mod_out_sem, mod_in_sem,
 ):
     width = stale_ref.shape[1]
     ff = wg.shape[1]
@@ -62,8 +63,12 @@
 
     loads = [
         pltpu.make_async_copy(src, dst, w_sem.at[i])
-        for i, (src, dst) in enumerate(((wg_hbm, wg), (wu_hbm, wu), (wd_hbm, wd)))
+        for i, (src, dst) in enumerate(
+            ((wg_hbm, wg), (wu_hbm, wu), (wd_hbm, wd), (mw_hbm, mw))
+        )
     ]
+    for i in (3, 0, 1, 2):
+        loads[i].start()
 
     def target(k):
         far = (1 - side) * half + (place + k) % half
@@ -99,6 +104,19 @@
             device_id_type=MESH,
         )
 
+    def strip(d):
+        return pl.ds(pl.multiple_of(d * 8, 8), 8)
+
+    def modward(k):
+        return pltpu.make_async_remote_copy(
+            src_ref=mod_own,
+            dst_ref=mod_all.at[strip(me)],
+            send_sem=mod_out_sem.at[k],
+            recv_sem=mod_in_sem.at[me],
+            device_id=(mine, target(k)),
+            device_id_type=MESH,
+        )
+
     barrier = pltpu.get_barrier_semaphore()
 
     @pl.loop(1, n)
@@ -107,7 +125,7 @@
             barrier, inc=1, device_id=(mine, (me + t) % n), device_id_type=MESH
         )
 
-    _, main, rest = keys_of(ids_ref[...])
+    hot, main, rest = keys_of(ids_ref[...])
     stale = stale_ref[...]
     table = lax.broadcasted_iota(jnp.int32, (stale.shape[0], EXPERTS * BASE), 1)
     over_rows = (((0,), (0,)), ((), ()))
@@ -138,9 +156,23 @@
     def _(k):
         outward(k).start()
 
-    for load in loads:
-        load.start()
     recv[pl.ds(half * BASE, BASE), :] = send[rows(me // group), :]
+
+    loads[3].wait()
+    conditioned = jax.nn.silu(cond_ref[...]).astype(jnp.bfloat16)
+    piece = bias_ref.shape[1]
+    own = jnp.dot(conditioned, mw[...], preferred_element_type=jnp.float32) + bias_ref[...]
+    mod_own[...] = jnp.zeros(mod_own.shape, jnp.float32)
+    mod_own[0:1, :piece] = own
+    mod_all[strip(me), :] = mod_own[...]
+
+    @pl.loop(0, half)
+    def _(k):
+        modward(k).start()
+
+    @pl.loop(half + 1, n)
+    def _(k):
+        modward(k).start()
 
     def work(c):
         base = c * per * BASE
@@ -217,6 +249,33 @@
     def _(t):
         d = (me + t) % n
         pltpu.make_async_remote_copy(
+            src_ref=mod_own,
+            dst_ref=mod_all.at[strip(d)],
+            send_sem=mod_out_sem.at[0],
+            recv_sem=mod_in_sem.at[d],
+            device_id=(mine, d),
+            device_id_type=MESH,
+        ).wait_recv()
+
+    stream = hidden_ref[...].astype(jnp.float32)
+    centered = stream - jnp.mean(stream, axis=-1, keepdims=True)
+    variance = jnp.mean(centered * centered, axis=-1, keepdims=True)
+    normed = centered * lax.rsqrt(variance + 1e-06)
+    modulation = jnp.concatenate([mod_all[d * 8 : d * 8 + 1, :piece] for d in range(n)], axis=1)
+    shift = modulation[:, :width]
+    scale = modulation[:, width : 2 * width]
+    current = (normed * (1.0 + scale) + shift).astype(jnp.bfloat16)
+    logits = jnp.dot(current, router_ref[...], preferred_element_type=jnp.float32)
+    picked = [jnp.sum(hot[k] * logits, axis=1, keepdims=True) for k in range(TOP)]
+    weights = [jax.nn.sigmoid(picked[k] - picked[1 - k]) for k in range(TOP)]
+    row = lax.broadcasted_iota(jnp.int32, (stream.shape[0], n * BASE), 1)
+    table = (row // (BASE * group)) * BASE + row % BASE
+    whole = [onehot(main[k], table) for k in range(TOP)]
+
+    @pl.loop(1, n)
+    def _(t):
+        d = (me + t) % n
+        pltpu.make_async_remote_copy(
             src_ref=ret.at[rows(0)],
             dst_ref=out_ref.at[rows(d)],
             send_sem=back_sem.at[0],
@@ -225,44 +284,28 @@
             device_id_type=MESH,
         ).wait_recv()
 
-    for low, high in ((0, half), (half + 1, n)):
-
-        @pl.loop(low, high)
-        def _(k):
-            outward(k).wait_send()
-            homeward(k).wait_send()
-
-
-def combine(group, ids_ref, hidden_ref, mod_ref, router_ref, back_ref, mixed_ref):
-    width = hidden_ref.shape[1]
-    stream = hidden_ref[...].astype(jnp.float32)
-    centered = stream - jnp.mean(stream, axis=-1, keepdims=True)
-    variance = jnp.mean(centered * centered, axis=-1, keepdims=True)
-    normed = centered * lax.rsqrt(variance + 1e-06)
-    shift = mod_ref[:, :width]
-    scale = mod_ref[:, width : 2 * width]
-    current = (normed * (1.0 + scale) + shift).astype(jnp.bfloat16)
-    logits = jnp.dot(current, router_ref[...], preferred_element_type=jnp.float32)
-    hot, main, rest = keys_of(ids_ref[...])
-    picked = [jnp.sum(hot[k] * logits, axis=1, keepdims=True) for k in range(TOP)]
-    row = lax.broadcasted_iota(jnp.int32, (stream.shape[0], back_ref.shape[0]), 1)
-    table = (row // (BASE * group)) * BASE + row % BASE
-    weights = [jax.nn.sigmoid(picked[k] - picked[1 - k]) for k in range(TOP)]
-    whole = [onehot(main[k], table) for k in range(TOP)]
     for q, first, size in pieces(width):
         cols = slice(first, first + size)
         routed = jnp.zeros((stream.shape[0], size), jnp.float32)
         for k in range(TOP):
-            found = jnp.dot(whole[k], back_ref[:, cols], preferred_element_type=jnp.float32)
+            found = jnp.dot(whole[k], out_ref[:, cols], preferred_element_type=jnp.float32)
             found = found + jnp.dot(
-                onehot(rest[k] + q * REST, table), back_ref[:, width : width + size],
+                onehot(rest[k] + q * REST, table), out_ref[:, width : width + size],
                 preferred_element_type=jnp.float32,
             )
             routed = routed + weights[k] * found
-        gate = mod_ref[:, 2 * width + first : 2 * width + first + size]
+        gate = modulation[:, 2 * width + first : 2 * width + first + size]
         mixed_ref[:, cols] = (hidden_ref[:, cols].astype(jnp.float32) + gate * routed).astype(
             mixed_ref.dtype
         )
+
+    for low, high in ((0, half), (half + 1, n)):
+
+        @pl.loop(low, high)
+        def _(k):
+            outward(k).wait_send()
+            modward(k).wait_send()
+            homeward(k).wait_send()
 
 
 def local(
@@ -275,27 +318,32 @@
     d_tile = 256
     message = width + PIECE
     per = n // CHUNKS
-    conditioned = jax.nn.silu(condition).astype(jnp.bfloat16)[None, :]
-    mod_piece = jnp.dot(conditioned, mod_weight, preferred_element_type=jnp.float32)[0] + mod_bias
-    modulation = lax.all_gather(mod_piece, "seq", axis=0, tiled=True)
+    piece = mod_bias.shape[0]
+    lanes = -(-piece // 128) * 128
     vmem = pl.BlockSpec(memory_space=pltpu.VMEM)
     hbm = pl.BlockSpec(memory_space=pl.ANY)
     bf16 = jnp.bfloat16
-    back = pl.pallas_call(
+    return pl.pallas_call(
         functools.partial(exchange, n, ff_tile, d_tile),
-        out_shape=jax.ShapeDtypeStruct((n * BASE, message), bf16),
-        in_specs=[vmem, vmem, hbm, hbm, hbm],
+        out_shape=jax.ShapeDtypeStruct(hidden_now.shape, hidden_now.dtype),
+        in_specs=[vmem] * 6 + [hbm] * 4,
         out_specs=vmem,
         scratch_shapes=[
+            pltpu.VMEM(mod_weight.shape, bf16),
             pltpu.VMEM(w_gate.shape, bf16),
             pltpu.VMEM(w_up.shape, bf16),
             pltpu.VMEM(w_down.shape, bf16),
             pltpu.VMEM((EXPERTS * BASE, message), bf16),
             pltpu.VMEM((n * BASE, message), bf16),
             pltpu.VMEM((n * BASE, message), bf16),
+            pltpu.VMEM((n * BASE, message), bf16),
             pltpu.VMEM((per * CAP, width), bf16),
             pltpu.VMEM((per * CAP, ff), bf16),
-            pltpu.SemaphoreType.DMA((3,)),
+            pltpu.VMEM((8, lanes), jnp.float32),
+            pltpu.VMEM((n * 8, lanes), jnp.float32),
+            pltpu.SemaphoreType.DMA((4,)),
+            pltpu.SemaphoreType.DMA((n,)),
+            pltpu.SemaphoreType.DMA((n,)),
             pltpu.SemaphoreType.DMA((n,)),
             pltpu.SemaphoreType.DMA((n,)),
             pltpu.SemaphoreType.DMA((n,)),
@@ -308,15 +356,10 @@
             flops=6 * n * CAP * width * ff, bytes_accessed=6 * width * ff, transcendentals=0
         ),
         name="exchange",
-    )(expert_ids, stale_rows, w_gate, w_up, w_down)
-    return pl.pallas_call(
-        functools.partial(combine, n // EXPERTS),
-        out_shape=jax.ShapeDtypeStruct(hidden_now.shape, hidden_now.dtype),
-        in_specs=[vmem] * 5,
-        out_specs=vmem,
-        compiler_params=pltpu.CompilerParams(vmem_limit_bytes=48 * 1024 * 1024),
-        name="combine",
-    )(expert_ids, hidden_now, modulation[None, :], router, back)
+    )(
+        expert_ids, stale_rows, hidden_now, condition[None, :], mod_bias[None, :], router,
+        mod_weight, w_gate, w_up, w_down,
+    )
 
 
 def solution(mesh):

time: 138 us -> 86.9 us (0.63)
  the two profiles are of different devices: /device:TPU:1 before, /device:TPU:24 now
where the time goes in v2:
time: 86.9 us; the launch traced here: 86.6 us
  Pallas kernels  76.5 us (88%)
  local copies, waits for them, and re-layouts  10.1 us (12%)
    pallas_call x1, Pallas kernels, local(): pl.pallas_call(functools.partial(exchange, n, ff_tile, d_tile), out_shape...  76.5 us
    unnamed x4, local copies, waits for them, and re-layouts  7.49 us

profile of v2, /device:TPU:24, one launch (start us, length us, event | category | flops | bytes accessed | tf_op | source)
XLA Modules:
  0.0 86.6 jit_solution(14830600194610901700)
XLA Ops:
  0.0 1.3 %broadcast_in_dim.7.bias_ref = f32[1,336]{1,0:T(1,128)} reshape(f32[336]{0:T(512)} %param.15) | data formatting | bytes 2688 | tf_op jit(solution)/shard_map/broadcast_in_dim | solution.py:360
  1.3 1.3 %broadcast_in_dim.6.cond_ref = f32[1,1792]{1,0:T(1,128)} reshape(f32[1792]{0:T(1024)} %param.13) | data formatting | bytes 14336 | tf_op jit(solution)/shard_map/broadcast_in_dim | solution.py:360
  2.6 1.4 %copy.11.ids_ref = s32[128,2]{1,0:T(8,128)} copy(s32[128,2]{0,1:T(2,128)} %param.12) | data formatting | bytes 2048 | tf_op args[2]
  4.0 1.8 %copy.12.router_ref = bf16[1792,16]{1,0:T(8,128)(2,1)} copy(bf16[1792,16]{0,1:T(8,128)(2,1)} %param.16) | data formatting | bytes 114688 | tf_op args[6]
  5.8 2.5 %copy.13.mw_hbm = bf16[1792,336]{1,0:T(8,128)(2,1)} copy(bf16[1792,336]{0,1:T(8,128)(2,1)} %param.14) | data formatting | bytes 2408448 | tf_op args[4]
  8.2 76.5 %exchange.1 = bf16[128,1792]{1,0:T(8,128)(2,1)} custom-call(s32[128,2]{1,0:T(8,128)} %copy.11.ids_ref, bf16[128,1792]{1,0:T(8,128)(2,1)} %stale_ref.1, bf16[128,1792]{1,0:T(8,128)(2,1)} %hidden_ref.1, f32[1,1792]{1,0:T(1,128)} %broadcast_in_dim.6.cond_ref, f32[1,336]{1,0:T(1,128)} %broadcast_in_dim.7.bias_ref, bf16[1792,16]{1,0:T(8,128)(2,1)} %copy.12.router_ref, ...), custom_call_target="tpu_custom_call" | custom-call | flops 12331253760 | bytes 38535168 | tf_op jit(solution)/shard_map/exchange/pallas_call | solution.py:326
  84.8 1.8 %copy.15 = bf16[128,1792]{1,0:T(8,128)(2,1)} copy(bf16[128,1792]{1,0:T(8,128)(2,1)} %exchange.1) | data formatting | bytes 917504

commit v3 on v2

--- a/solution.py
+++ b/solution.py
@@ -14,7 +14,7 @@
 REST = CAP - BASE
 PARTS = BASE // REST
 PIECE = 512
-CHUNKS = 4
+CHUNKS = 2
 MESH = pl.DeviceIdType.MESH
 
 
@@ -23,20 +23,20 @@
 
 
 def keys_of(ids):
-    rows = ids.shape[0]
-    experts = lax.broadcasted_iota(jnp.int32, (rows, EXPERTS), 1)
-    hot = [(ids[:, k : k + 1] == experts).astype(jnp.float32) for k in range(TOP)]
-    below = (
-        lax.broadcasted_iota(jnp.int32, (rows, rows), 1)
-        < lax.broadcasted_iota(jnp.int32, (rows, rows), 0)
-    ).astype(jnp.bfloat16)
+    rows = ids.shape[1]
+    experts = lax.broadcasted_iota(jnp.int32, (EXPERTS, rows), 0)
+    hot = [(ids[k : k + 1, :] == experts).astype(jnp.float32) for k in range(TOP)]
+    earlier = (
+        lax.broadcasted_iota(jnp.int32, (rows, rows), 0)
+        < lax.broadcasted_iota(jnp.int32, (rows, rows), 1)
+    ).astype(jnp.float32).astype(jnp.bfloat16)
     before = jnp.dot(
-        below, (hot[0] + hot[1]).astype(jnp.bfloat16), preferred_element_type=jnp.float32
+        (hot[0] + hot[1]).astype(jnp.bfloat16), earlier, preferred_element_type=jnp.float32
     )
     main, rest = [], []
     for k in range(TOP):
-        slot = jnp.sum(hot[k] * before, axis=1, keepdims=True).astype(jnp.int32)
-        first = ids[:, k : k + 1] * BASE + slot
+        slot = jnp.sum(hot[k] * before, axis=0, keepdims=True).astype(jnp.int32)
+        first = ids[k : k + 1, :] * BASE + slot
         main.append(jnp.where(slot < BASE, first, -1))
         rest.append(jnp.where(slot >= BASE, first - BASE, -(EXPERTS + 1) * BASE))
     return hot, main, rest
@@ -127,17 +127,17 @@
 
     hot, main, rest = keys_of(ids_ref[...])
     stale = stale_ref[...]
-    table = lax.broadcasted_iota(jnp.int32, (stale.shape[0], EXPERTS * BASE), 1)
+    table = lax.broadcasted_iota(jnp.int32, (EXPERTS * BASE, stale.shape[0]), 0)
     over_rows = (((0,), (0,)), ((), ()))
     pick = onehot(main[0], table) + onehot(main[1], table)
-    send[:, :width] = lax.dot_general(
-        pick, stale, over_rows, preferred_element_type=jnp.float32
+    send[:, :width] = jnp.dot(
+        pick, stale, preferred_element_type=jnp.float32
     ).astype(jnp.bfloat16)
     tail = jnp.zeros((EXPERTS * BASE, PIECE), jnp.float32)
     for q, first, size in pieces(width):
         pick = onehot(rest[0] + q * REST, table) + onehot(rest[1] + q * REST, table)
-        part = lax.dot_general(
-            pick, stale[:, first : first + size], over_rows, preferred_element_type=jnp.float32
+        part = jnp.dot(
+            pick, stale[:, first : first + size], preferred_element_type=jnp.float32
         )
         if size < PIECE:
             part = jnp.concatenate(
@@ -159,9 +159,12 @@
     recv[pl.ds(half * BASE, BASE), :] = send[rows(me // group), :]
 
     loads[3].wait()
-    conditioned = jax.nn.silu(cond_ref[...]).astype(jnp.bfloat16)
-    piece = bias_ref.shape[1]
-    own = jnp.dot(conditioned, mw[...], preferred_element_type=jnp.float32) + bias_ref[...]
+    conditioned = jax.nn.silu(cond_ref[...].reshape(1, -1)).astype(jnp.bfloat16)
+    piece = bias_ref.shape[0]
+    over_features = (((1,), (1,)), ((), ()))
+    own = lax.dot_general(
+        conditioned, mw[...], over_features, preferred_element_type=jnp.float32
+    ) + bias_ref[...].reshape(1, -1)
     mod_own[...] = jnp.zeros(mod_own.shape, jnp.float32)
     mod_own[0:1, :piece] = own
     mod_all[strip(me), :] = mod_own[...]
@@ -265,10 +268,15 @@
     shift = modulation[:, :width]
     scale = modulation[:, width : 2 * width]
     current = (normed * (1.0 + scale) + shift).astype(jnp.bfloat16)
-    logits = jnp.dot(current, router_ref[...], preferred_element_type=jnp.float32)
-    picked = [jnp.sum(hot[k] * logits, axis=1, keepdims=True) for k in range(TOP)]
-    weights = [jax.nn.sigmoid(picked[k] - picked[1 - k]) for k in range(TOP)]
-    row = lax.broadcasted_iota(jnp.int32, (stream.shape[0], n * BASE), 1)
+    logits = lax.dot_general(
+        router_ref[...], current, over_features, preferred_element_type=jnp.float32
+    )
+    picked = [jnp.sum(hot[k] * logits, axis=0, keepdims=True) for k in range(TOP)]
+    weights = [
+        jnp.broadcast_to(jax.nn.sigmoid(picked[k] - picked[1 - k]), (128, stream.shape[0])).T[:, :1]
+        for k in range(TOP)
+    ]
+    row = lax.broadcasted_iota(jnp.int32, (n * BASE, stream.shape[0]), 0)
     table = (row // (BASE * group)) * BASE + row % BASE
     whole = [onehot(main[k], table) for k in range(TOP)]
 
@@ -288,10 +296,12 @@
         cols = slice(first, first + size)
         routed = jnp.zeros((stream.shape[0], size), jnp.float32)
         for k in range(TOP):
-            found = jnp.dot(whole[k], out_ref[:, cols], preferred_element_type=jnp.float32)
-            found = found + jnp.dot(
+            found = lax.dot_general(
+                whole[k], out_ref[:, cols], over_rows, preferred_element_type=jnp.float32
+            )
+            found = found + lax.dot_general(
                 onehot(rest[k] + q * REST, table), out_ref[:, width : width + size],
-                preferred_element_type=jnp.float32,
+                over_rows, preferred_element_type=jnp.float32,
             )
             routed = routed + weights[k] * found
         gate = modulation[:, 2 * width + first : 2 * width + first + size]
@@ -329,7 +339,7 @@
         in_specs=[vmem] * 6 + [hbm] * 4,
         out_specs=vmem,
         scratch_shapes=[
-            pltpu.VMEM(mod_weight.shape, bf16),
+            pltpu.VMEM(mod_weight.shape[::-1], bf16),
             pltpu.VMEM(w_gate.shape, bf16),
             pltpu.VMEM(w_up.shape, bf16),
             pltpu.VMEM(w_down.shape, bf16),
@@ -357,8 +367,8 @@
         ),
         name="exchange",
     )(
-        expert_ids, stale_rows, hidden_now, condition[None, :], mod_bias[None, :], router,
-        mod_weight, w_gate, w_up, w_down,
+        expert_ids.T, stale_rows, hidden_now, condition, mod_bias, router.T,
+        mod_weight.T, w_gate, w_up, w_down,
     )
 
 

time: 86.9 us -> 72.7 us (0.84)
  the two profiles are of different devices: /device:TPU:24 before, /device:TPU:1 now
where the time goes in v3:
time: 72.7 us; the launch traced here: 72.5 us
  Pallas kernels  70.7 us (97%)
  local copies, waits for them, and re-layouts  1.82 us (3%)
    pallas_call x1, Pallas kernels, local(): pl.pallas_call(functools.partial(exchange, n, ff_tile, d_tile), out_shape...  70.7 us
    unnamed x1, local copies, waits for them, and re-layouts  1.82 us

profile of v3, /device:TPU:1, one launch (start us, length us, event | category | flops | bytes accessed | tf_op | source)
XLA Modules:
  0.0 72.5 jit_solution(4455661936101722654)
XLA Ops:
  0.0 70.7 %exchange.1 = bf16[128,1792]{1,0:T(8,128)(2,1)} custom-call(s32[2,128]{1,0:T(2,128)} %bitcast.5, bf16[128,1792]{1,0:T(8,128)(2,1)} %stale_ref.1, bf16[128,1792]{1,0:T(8,128)(2,1)} %hidden_ref.1, f32[1792]{0:T(1024)} %cond_ref.1, f32[336]{0:T(512)} %bias_ref.1, bf16[16,1792]{1,0:T(8,128)(2,1)} %bitcast.4, bf16[336,1792]{1,0:T(8,128)(2,1)} %bitcast.3, ...), custom_call_target="tpu_custom_call" | custom-call | flops 12331253760 | bytes 38535168 | tf_op jit(solution)/shard_map/exchange/pallas_call | solution.py:336
  70.7 1.8 %copy.12 = bf16[128,1792]{1,0:T(8,128)(2,1)} copy(bf16[128,1792]{1,0:T(8,128)(2,1)} %exchange.1) | data formatting | bytes 917504

commit v4 on v3

--- a/solution.py
+++ b/solution.py
@@ -14,7 +14,7 @@
 REST = CAP - BASE
 PARTS = BASE // REST
 PIECE = 512
-CHUNKS = 2
+CHUNKS = ((0, 4), (8, 8), (4, 4))
 MESH = pl.DeviceIdType.MESH
 
 
@@ -56,7 +56,6 @@
     ff = wg.shape[1]
     group = n // EXPERTS
     half = n // 2
-    per = n // CHUNKS
     me = lax.axis_index("seq")
     mine = lax.axis_index("groups")
     side, place = me // half, me % half
@@ -148,7 +147,7 @@
 
     pl.semaphore_wait(barrier, n - 1)
 
-    @pl.loop(0, half)
+    @pl.loop(0, half // 2)
     def _(k):
         outward(k).start()
 
@@ -177,40 +176,49 @@
     def _(k):
         modward(k).start()
 
-    def work(c):
-        base = c * per * BASE
+    @pl.loop(0, half // 2)
+    def _(k):
+        outward(k).wait_send()
+
+    @pl.loop(half // 2, half)
+    def _(k):
+        outward(k).start()
+
+    def work(low, per, is_first):
+        base = low * BASE
         count = per * BASE
         extra = per * REST
         got = pl.ds(base, count)
+        used = pl.ds(0, count + extra)
         xbuf[:count] = recv[got, :width]
         across = lax.broadcasted_iota(jnp.int32, (extra, count), 1)
         down = lax.broadcasted_iota(jnp.int32, (extra, count), 0)
         spread = (down // REST) * BASE + down % REST
         tails = recv[got, width:]
         for q, first, size in pieces(width):
-            xbuf[count:, first : first + size] = jnp.dot(
+            xbuf[count : count + extra, first : first + size] = jnp.dot(
                 onehot(spread + q * REST, across), tails[:, :size],
                 preferred_element_type=jnp.float32,
             ).astype(jnp.bfloat16)
-        if c == 0:
+        if is_first:
             loads[0].wait()
             loads[1].wait()
 
         @pl.loop(0, ff // ff_tile)
         def _(j):
             cols = pl.ds(pl.multiple_of(j * ff_tile, ff_tile), ff_tile)
-            gate = jnp.dot(xbuf[...], wg[:, cols], preferred_element_type=jnp.float32)
-            up = jnp.dot(xbuf[...], wu[:, cols], preferred_element_type=jnp.float32)
-            act[:, cols] = (jax.nn.silu(gate) * up).astype(jnp.bfloat16)
-
-        if c == 0:
+            gate = jnp.dot(xbuf[used, :], wg[:, cols], preferred_element_type=jnp.float32)
+            up = jnp.dot(xbuf[used, :], wu[:, cols], preferred_element_type=jnp.float32)
+            act[used, cols] = (jax.nn.silu(gate) * up).astype(jnp.bfloat16)
+
+        if is_first:
             loads[2].wait()
 
         @pl.loop(0, width // d_tile)
         def _(j):
             cols = pl.ds(pl.multiple_of(j * d_tile, d_tile), d_tile)
-            xbuf[:, cols] = jnp.dot(
-                act[...], wd[:, cols], preferred_element_type=jnp.float32
+            xbuf[used, cols] = jnp.dot(
+                act[used, :], wd[:, cols], preferred_element_type=jnp.float32
             ).astype(jnp.bfloat16)
 
         ret[got, :width] = xbuf[:count]
@@ -220,7 +228,7 @@
         back = jnp.zeros((count, PIECE), jnp.float32)
         for q, first, size in pieces(width):
             part = jnp.dot(
-                onehot(spread + q * REST, down), xbuf[count:, first : first + size],
+                onehot(spread + q * REST, down), xbuf[count : count + extra, first : first + size],
                 preferred_element_type=jnp.float32,
             )
             if size < PIECE:
@@ -230,22 +238,21 @@
             back = back + part
         ret[got, width:] = back.astype(jnp.bfloat16)
 
-    for c in range(CHUNKS):
-        low, high = c * per, (c + 1) * per
-        if low == half:
-            low = low + 1
-
-        @pl.loop(low, high)
+    for i, (begin, size) in enumerate(CHUNKS):
+        low, high = begin * n // 16, (begin + size) * n // 16
+        skip = 1 if low == half else 0
+
+        @pl.loop(low + skip, high)
         def _(k):
             outward(k).wait_recv()
 
-        work(c)
-
-        @pl.loop(low, high)
+        work(low, high - low, i == 0)
+
+        @pl.loop(low + skip, high)
         def _(k):
             homeward(k).start()
 
-        if c * per == half:
+        if skip:
             out_ref[rows(me), :] = ret[pl.ds(half * BASE, BASE), :]
 
     @pl.loop(1, n)
@@ -309,11 +316,16 @@
             mixed_ref.dtype
         )
 
-    for low, high in ((0, half), (half + 1, n)):
+    for low, high in ((half // 2, half), (half + 1, n)):
 
         @pl.loop(low, high)
         def _(k):
             outward(k).wait_send()
+
+    for low, high in ((0, half), (half + 1, n)):
+
+        @pl.loop(low, high)
+        def _(k):
             modward(k).wait_send()
             homeward(k).wait_send()
 
@@ -327,7 +339,7 @@
     ff_tile = 512 if ff % 512 == 0 else ff
     d_tile = 256
     message = width + PIECE
-    per = n // CHUNKS
+    per = max(size for _, size in CHUNKS) * n // 16
     piece = mod_bias.shape[0]
     lanes = -(-piece // 128) * 128
     vmem = pl.BlockSpec(memory_space=pltpu.VMEM)

time: 72.7 us -> 68.5 us (0.942)
  Pallas kernels: 70.7 us -> 66.1 us
    pallas_call x1, Pallas kernels: 70.7 us -> 66.1 us  [local(): pl.pallas_call(functools.partial(exchange, n, ff_tile, d_tile), out_shape...]
where the time goes in v4:
time: 68.5 us; the launch traced here: 67.9 us
  Pallas kernels  66.1 us (96%)
  local copies, waits for them, and re-layouts  1.82 us (3%)
    pallas_call x1, Pallas kernels, local(): pl.pallas_call(functools.partial(exchange, n, ff_tile, d_tile), out_shape...  66.1 us
    unnamed x1, local copies, waits for them, and re-layouts  1.82 us

profile of v4, /device:TPU:1, one launch (start us, length us, event | category | flops | bytes accessed | tf_op | source)
XLA Modules:
  0.0 67.9 jit_solution(12305775942514512333)
XLA Ops:
  0.0 66.1 %exchange.1 = bf16[128,1792]{1,0:T(8,128)(2,1)} custom-call(s32[2,128]{1,0:T(2,128)} %bitcast.5, bf16[128,1792]{1,0:T(8,128)(2,1)} %stale_ref.1, bf16[128,1792]{1,0:T(8,128)(2,1)} %hidden_ref.1, f32[1792]{0:T(1024)} %cond_ref.1, f32[336]{0:T(512)} %bias_ref.1, bf16[16,1792]{1,0:T(8,128)(2,1)} %bitcast.4, bf16[336,1792]{1,0:T(8,128)(2,1)} %bitcast.3, ...), custom_call_target="tpu_custom_call" | custom-call | flops 12331253760 | bytes 38535168 | tf_op jit(solution)/shard_map/exchange/pallas_call | solution.py:348
  66.1 1.8 %copy.12 = bf16[128,1792]{1,0:T(8,128)(2,1)} copy(bf16[128,1792]{1,0:T(8,128)(2,1)} %exchange.1) | data formatting | bytes 917504
